TPU v7x, 128 devices: a whole 4x4x4 slice. The times are simulated.
128 devices in a mesh: rep: 16 (over y, x_hi, core), fsdp: 8 (over z, x_lo).
Axes of the slice: x: 4 (x_hi: 2, x_lo: 2; x = x_hi * 2 + x_lo), y: 4, z: 4, core: 2. Of those that a mesh axis runs over, the one named last changes fastest.
Arguments:
- params: float32 [16, 2560, 2560], P('rep', 'fsdp'), may hold values from -6 to 6
- push_weight: float32 [16], P('rep'), may hold values from 0.5 to 2
- inbox_params: float32 [16, 2560, 2560], P('rep', 'fsdp'), may hold values from -3 to 3
- inbox_weight: float32 [16], P('rep'), may hold values from 0.25 to 1
- heads: bfloat16 [16, 3072, 2560], P('rep', 'fsdp'), may hold values from -6 to 6
- residual: bfloat16 [16, 3072, 2560], P('rep', 'fsdp'), may hold values from -40 to 40
- cotangent: bfloat16 [16, 3072, 2560], P('rep', 'fsdp'), may hold values from -6 to 6
- gain: float32 [2560], replicated, may hold values from 0.5 to 2
- offset: int32 [8], replicated, may hold values from 1 to 8, as said below
Outputs:
- new_params: float32 [16, 2560, 2560], P('rep', 'fsdp')
- new_weight: float32 [16], P('rep')
- outbox_params: float32 [16, 2560, 2560], P('rep', 'fsdp')
- outbox_weight: float32 [16], P('rep')
- grad_heads: bfloat16 [16, 3072, 2560], P('rep', 'fsdp')
Inputs may be any that keep to these rules, and one draw needn't show every extreme that they name: `offset`: each entry a power of two below 16; 1 and 8 both occur in every plan.
All inputs are finite; a program needn't handle non-finite values.
Results may differ from a plain program's by a relative error of at most 0.0057.
Values may be sent and summed in bfloat16 or wider, within the bound.
A program may use at most 192 MiB of HBM per device.

v0:
```python
from functools import partial

import jax
import jax.numpy as jnp
from jax import lax
from jax.sharding import PartitionSpec as P


def passed_along(value, axis, by):
    length = lax.axis_size(axis)
    return lax.ppermute(value, axis, [(i, (i + by) % length) for i in range(length)])


def deliver(payload, bit_place):
    return passed_along(payload, "rep", 1 << bit_place)


def local(
    params, push_weight, inbox_params, inbox_weight, heads, residual, cotangent, gain, offset
):
    numer = params[0]
    weight_one = push_weight[0]
    head_rows = heads[0]
    scaling = heads.shape[2] ** (-0.5)
    weights_shard = (numer / weight_one * scaling).astype(jnp.bfloat16)
    full_weights = lax.all_gather(weights_shard, "fsdp", axis=0, tiled=True)
    summed = residual[0].astype(jnp.float32) + jnp.dot(
        head_rows, full_weights, preferred_element_type=jnp.float32
    )
    inverse = lax.rsqrt(jnp.mean(summed * summed, axis=-1, keepdims=True) + 1e-05)
    scaled_cot = gain * cotangent[0].astype(jnp.float32)
    unit_grad = (
        inverse * scaled_cot
        - summed * inverse**3 * jnp.mean(scaled_cot * summed, axis=-1, keepdims=True)
    ).astype(jnp.bfloat16)
    grad_rows = lax.dot_general(
        unit_grad, full_weights, (((1,), (1,)), ((), ())), preferred_element_type=jnp.float32
    ).astype(jnp.bfloat16)
    weight_grad = lax.psum_scatter(
        lax.dot_general(
            head_rows, unit_grad, (((0,), (0,)), ((), ())), preferred_element_type=jnp.float32
        ).astype(jnp.bfloat16),
        "fsdp",
        scatter_dimension=0,
        tiled=True,
    ).astype(jnp.float32)
    kept_half = 0.5 * (numer - 0.004 * weight_grad)
    new_params = (kept_half + inbox_params[0])[None]
    new_weight = 0.5 * push_weight + inbox_weight
    levels = lax.axis_size("rep").bit_length() - 1
    powers = jnp.left_shift(jnp.ones((levels,), jnp.int32), jnp.arange(levels, dtype=jnp.int32))
    level_index = jnp.sum(jnp.where(powers == offset[0], jnp.arange(levels, dtype=jnp.int32), 0))
    payload = (kept_half[None], 0.5 * push_weight)
    branches = [partial(deliver, payload, bit_place) for bit_place in range(levels)]
    outbox_params, outbox_weight = lax.switch(level_index, branches)
    return (new_params, new_weight, outbox_params, outbox_weight, grad_rows[None])


def solution(mesh):
    placed = (
        P("rep", "fsdp", None),
        P("rep"),
        P("rep", "fsdp", None),
        P("rep"),
        P("rep", "fsdp", None),
        P("rep", "fsdp", None),
        P("rep", "fsdp", None),
        P(),
        P(),
    )
    return jax.shard_map(
        local,
        mesh=mesh,
        in_specs=placed,
        out_specs=(
            P("rep", "fsdp", None),
            P("rep"),
            P("rep", "fsdp", None),
            P("rep"),
            P("rep", "fsdp", None),
        ),
        check_vma=False,
    )
```

profile of v0, /device:TPU:0, one launch (start us, length us, event | category | flops | bytes accessed | tf_op | source)
XLA Modules:
  0.0 633.8 jit_solution(13243010801760944380)
XLA Ops:
  7.2 0.0 copy-start
  7.2 0.0 all-gather.2.cloned.1.call-start
  8.0 3.4 fusion.10
  11.4 0.0 all-gather.2.cloned.1.call-update
  11.4 0.0 copy-start.5
  11.4 0.0 reduce-scatter.4.cloned.1.call-start
  11.5 4.0 copy.24
  15.4 3.9 copy.23
  19.4 251.4 %all-gather.2.cloned.1.call-done = bf16[2560,2560]{1,0:T(8,128)(2,1)} async-done(((bf16[320,2560]{1,0:T(8,128)(2,1)}), bf16[2560,2560]{1,0:T(8,128)(2,1)}) %all-gather.2.cloned.1.call-update) | async-done | bytes 13107216 | tf_op jit(solution)/shard_map/all_gather | solution.py:26
  270.8 0.0 copy-done
  270.8 0.0 copy-done.5
  270.8 0.0 copy-start.2
  270.8 11.7 %multiply_reduce_fusion = (f32[384]{0:T(512)S(1)}, f32[384]{0:T(512)S(1)}, f32[384,2560]{0,1:T(8,128)S(1)}) fusion(bf16[1,384,2560]{1,2,0:T(8,128)(2,1)} %copy.24, f32[2560]{0:T(1024)S(1)} %copy-done.5, bf16[2560,2560]{1,0:T(8,128)(2,1)} %all-gather.2.cloned.1.call-done, bf16[1,384,2560]{2,1,0:T(8,128)(2,1)S(1)} %copy-done, bf16[1,384,2560]{1,2,0:T(8,128)(2,1)} %copy.23), kind=kOutput, calls=%fused_computation.11 | convolution fusion | flops 5041028096 | bytes 22950912 | tf_op jit(solution)/shard_map/dot_general | solution.py:27
  282.5 0.0 copy-done.2
  282.5 1.3 fusion.5
  283.9 0.0 copy-start.3
  283.9 1.3 copy-done.3
  285.1 10.0 %fusion = bf16[2560,2560]{0,1:T(8,128)(2,1)} fusion(bf16[384,2560]{0,1:T(8,128)(2,1)S(1)} %fusion.5, bf16[1,384,2560]{2,1,0:T(8,128)(2,1)S(1)} %copy-done), kind=kOutput, calls=%fused_computation.1 | convolution fusion | flops 5039718400 | bytes 17039360 | tf_op jit(solution)/shard_map/dot_general | solution.py:40
  295.2 17.6 %copy.26 = bf16[2560,2560]{1,0:T(8,128)(2,1)} copy(bf16[2560,2560]{0,1:T(8,128)(2,1)} %fusion) | data formatting | bytes 26214400
  312.8 0.0 copy-start.6
  312.8 0.0 copy-start.4
  312.8 0.0 reduce-scatter.4.cloned.1.call-update
  313.6 0.0 copy-done.6
  313.6 0.7 fusion.15
  314.9 0.0 copy-done.4
  314.9 10.1 %fusion.7 = bf16[1,384,2560]{2,1,0:T(8,128)(2,1)} fusion(bf16[384,2560]{0,1:T(8,128)(2,1)S(1)} %copy-done.4, bf16[2560,2560]{1,0:T(8,128)(2,1)} %all-gather.2.cloned.1.call-done), kind=kOutput, calls=%fused_computation.12 | convolution fusion | flops 5034147840 | bytes 17039360 | tf_op jit(solution)/shard_map/dot_general | solution.py:36
  325.0 247.0 %reduce-scatter.4.cloned.1.call-done = bf16[320,2560]{1,0:T(8,128)(2,1)} async-done(((bf16[2560,2560]{1,0:T(8,128)(2,1)}), bf16[320,2560]{1,0:T(8,128)(2,1)}) %reduce-scatter.4.cloned.1.call-update) | async-done | bytes 1638416 | tf_op jit(solution)/shard_map/reduce_scatter | solution.py:39
  572.0 6.2 fusion.14
  578.2 41.9 %conditional.1 = (f32[1,320,2560]{2,1,0:T(8,128)}, f32[1]{0:T(128)}) conditional(s32[]{:T(128)} %clamp.3, (f32[1,320,2560]{2,1,0:T(8,128)S(1)}, f32[1]{0:T(128)}) %tuple.24, (f32[1,320,2560]{2,1,0:T(8,128)S(1)}, f32[1]{0:T(128)}) %tuple.24, (f32[1,320,2560]{2,1,0:T(8,128)S(1)}, f32[1]{0:T(128)}) %tuple.24, ...), branch_computations={%region_4.5_spmd, %region_5.6_spmd, %region_6.7_spmd, %region_7.8_... | conditional | bytes 13107312 | solution.py:55
  578.2 0.0 collective-permute-start
  578.2 5.6 collective-permute-start.1
  583.8 36.3 %collective-permute-done.1 = f32[1]{0:T(128)} collective-permute-done((f32[1]{0:T(128)}, f32[1]{0:T(128)}, u32[]{:S(2)}, u32[]{:S(2)}) %collective-permute-start.1) | collective-permute-done | bytes 36 | tf_op jit(solution)/shard_map/cond/branch_0_fun/ppermute | solution.py:11
  620.1 0.0 collective-permute-done
  620.1 0.0 copy-start.1
  620.1 4.0 copy.40
  624.7 0.0 copy-done.1
  (1 shorter events, 0.0 us)
Async XLA Ops:
  7.2 263.6 %copy-start = (bf16[1,384,2560]{2,1,0:T(8,128)(2,1)S(1)}, bf16[1,384,2560]{2,1,0:T(8,128)(2,1)}, u32[]{:S(2)}) copy-start(bf16[1,384,2560]{2,1,0:T(8,128)(2,1)} %param.17) | copy-start | bytes 5898244
  7.2 263.6 %all-gather.2.cloned.1.call-start = ((), (), s32[]{:S(2)}) async-start(), calls=%async_computation.1 | async-start | bytes 14745600 | tf_op jit(solution)/shard_map/all_gather | solution.py:26
  11.4 259.4 %copy-start.5 = (f32[2560]{0:T(1024)S(1)}, f32[2560]{0:T(1024)}, u32[]{:S(2)}) copy-start(f32[2560]{0:T(1024)} %param.20) | copy-start | bytes 30724
  11.4 560.6 %reduce-scatter.4.cloned.1.call-start = ((), (), s32[]{:S(2)}) async-start(), calls=%async_computation.2 | async-start | bytes 14745600 | tf_op jit(solution)/shard_map/reduce_scatter | solution.py:39
  270.8 11.7 %copy-start.2 = (bf16[1,384,2560]{1,2,0:T(8,128)(2,1)S(1)}, bf16[1,384,2560]{1,2,0:T(8,128)(2,1)}, u32[]{:S(2)}) copy-start(bf16[1,384,2560]{1,2,0:T(8,128)(2,1)} %copy.24) | copy-start | bytes 5898244
  283.9 1.3 copy-start.3
  312.8 0.8 copy-start.6
  312.8 2.2 copy-start.4
  578.2 41.9 %collective-permute-start = (f32[1,320,2560]{2,1,0:T(8,128)S(1)}, f32[1,320,2560]{2,1,0:T(8,128)}, u32[]{:S(2)}, u32[]{:S(2)}) collective-permute-start(f32[1,320,2560]{2,1,0:T(8,128)S(1)} %get-tuple-element.16), channel_id=1, source_target_pairs={{0,8},{8,16},{16,24},{24,32},{32,40},{40,48},{48,56},{56,64},{64,7... | collective-permute-start | bytes 9830408 | tf_op jit(solution)/shard_map/cond/branch_0_fun/ppermute | solution.py:11
  578.2 41.9 %collective-permute-start.1 = (f32[1]{0:T(128)}, f32[1]{0:T(128)}, u32[]{:S(2)}, u32[]{:S(2)}) collective-permute-start(f32[1]{0:T(128)} %get-tuple-element.17), channel_id=1, source_target_pairs={{0,8},{8,16},{16,24},{24,32},{32,40},{40,48},{48,56},{56,64},{64,7... | collective-permute-start | bytes 20 | tf_op jit(solution)/shard_map/cond/branch_0_fun/ppermute | solution.py:11
  620.1 4.6 copy-start.1
Sparse Core Ops, SparseCore 0:
  11.5 259.2 all-gather.1
  312.9 259.0 reduce-scatter.3
where the time goes:
time: 635 us; the launch traced here: 634 us
  waiting for transfers between devices  535 us (84%)
  matrix products  31.8 us (5%)
  local copies, waits for them, and re-layouts  30.8 us (5%)
  between operations  19.2 us (3%)
  other arithmetic  11.6 us (2%)
    all_gather x1, waiting for transfers between devices, local(): full_weights = lax.all_gather(weights_shard, 'fsdp', axis=0, tiled=True)  251 us
    reduce_scatter x1, waiting for transfers between devices, local(): lax.psum_scatter(lax.dot_general(head_rows, unit_grad, (((0,), (0,)), (()...  247 us
    ppermute x2, waiting for transfers between devices, passed_along(): lax.ppermute(value, axis, [(i, (i + by) % length) for i in range(length)])  36.3 us
    unnamed x18, local copies, waits for them, and re-layouts  30.8 us
  transfers between devices with their start and end apart: 4, of which 3 were waited for; matrix products, arithmetic and copies ran while one was open for 3% of the time, Pallas kernels for 0%

commit v1 on v0

v1 whole, which is shorter than its diff:
```python
import functools

import jax
import jax.numpy as jnp
from jax import lax
from jax.experimental import pallas as pl
from jax.experimental.pallas import tpu as pltpu
from jax.sharding import PartitionSpec as P

MESH = pl.DeviceIdType.MESH
F32 = jnp.float32
BF16 = jnp.bfloat16

CW = 256
PIECES = 4
LEAD = 4
EPS = 1e-05


def dot(a, b):
    return jnp.dot(a, b, preferred_element_type=F32)


def dot_t(a, b):
    return lax.dot_general(a, b, (((1,), (1,)), ((), ())), preferred_element_type=F32)


def step_kernel(
    by, zs, inner,
    params, push, heads, residual, cotangent, gain,
    g_own, g_got, dw_out, outbox, w_out,
    pv, hv, rv, cv, hp, ho, ht, wb, sv, sb, srv, acc1, acc2, ub, pb, st1, st2, gacc, gb, gsend, ob, dwv, wv,
    lp, lx, hs, hr, aos, aor, afs, afr, ss, sr, us, ur, s1s, s1r, s2s, s2r, gs, gr, os_, or_, ws, wr, dws, gos,
):
    rows, cols = params.shape
    tok = heads.shape[0]
    nc = cols // CW
    half = rows // 2
    kh = zs * rows
    reps = lax.axis_size("rep")
    r = lax.axis_index("rep")
    f = lax.axis_index("fsdp")
    z, xl = f // 2, f % 2
    zp, zm, zo = (z + 1) % zs, (z + zs - 1) % zs, (z + 2) % zs
    up, down = (r, zp * 2 + xl), (r, zm * 2 + xl)
    side = (r, z * 2 + 1 - xl)
    ahead, behind = ((r + by) % reps, f), ((r + reps - by) % reps, f)
    ways = (up, down)

    def remote(src, dst, send, recv, to):
        return pltpu.make_async_remote_copy(
            src_ref=src, dst_ref=dst, send_sem=send, recv_sem=recv, device_id=to, device_id_type=MESH
        )

    def at_cols(c):
        return pl.ds(pl.multiple_of(c * CW, CW), CW)

    def at_rows(start, size):
        return pl.ds(pl.multiple_of(start, 16), size)

    def load_params(c):
        return pltpu.make_async_copy(params.at[:, at_cols(c)], pv.at[c], lp.at[c])

    load_heads = pltpu.make_async_copy(heads, hv, lx.at[0])
    load_res = pltpu.make_async_copy(residual, rv, lx.at[1])
    load_cot = pltpu.make_async_copy(cotangent, cv, lx.at[2])
    piece = tok // PIECES

    def send_heads(p):
        here = at_rows(p * piece, piece)
        there = at_rows(tok + p * piece, piece)
        return remote(ho.at[here], hp.at[there], hs.at[p], hr.at[p], side)

    def send_own(d, c):
        block = wb.at[c, at_rows(z * rows, rows)]
        return remote(block, block, aos.at[d, c], aor.at[d, c], ways[d])

    def send_on(d, c):
        start = zm * rows if d == 0 else zp * rows + half
        block = wb.at[c, at_rows(start, half)]
        return remote(block, block, afs.at[d, c], afr.at[d, c], ways[d])

    def send_sum(c):
        return remote(sb.at[c], srv.at[c], ss.at[c], sr.at[c], side)

    def send_unit(c):
        return remote(ub.at[c, pl.ds(0, tok)], ub.at[c, pl.ds(tok, tok)], us.at[c], ur.at[c], side)

    def send_far(d, c):
        block = pb.at[c, at_rows(zo * rows + d * half, half)]
        return remote(block, st1.at[d, c], s1s.at[d, c], s1r.at[d, c], ways[d])

    def send_near(d, c):
        block = pb.at[c, at_rows((zm if d else zp) * rows, rows)]
        return remote(block, st2.at[d, c], s2s.at[d, c], s2r.at[d, c], ways[d])

    def send_grad(p):
        here = at_rows(p * piece, piece)
        return remote(gsend.at[here], g_got.at[here], gs.at[p], gr.at[p], side)

    def send_out(c):
        return remote(ob.at[c], outbox.at[:, at_cols(c)], os_.at[c], or_.at[c], ahead)

    send_weight = remote(wv, w_out, ws.at[0], wr.at[0], ahead)

    def store_dw(c):
        return pltpu.make_async_copy(dwv.at[c], dw_out.at[:, at_cols(c)], dws.at[c])

    store_own = pltpu.make_async_copy(gb, g_own, gos.at[0])

    def loads(c, _):
        load_params(c).start()
        return 0

    lax.fori_loop(0, nc, loads, 0)
    load_heads.start()
    load_res.start()
    load_cot.start()

    barrier = pltpu.get_barrier_semaphore()
    for device in (up, down, side, ahead, behind):
        pl.semaphore_signal(barrier, inc=1, device_id=device, device_id_type=MESH)
    pl.semaphore_wait(barrier, 5)

    weight = push[0]
    scale = (inner ** -0.5) / jnp.full((1, CW), weight, F32)

    def own_chunk(c):
        load_params(c).wait()
        wb[c, at_rows(z * rows, rows), :] = (pv[c] * scale).astype(BF16)
        for d in range(2):
            send_own(d, c).start()

    own_chunk(0)
    load_heads.wait()

    def split_heads(p, _):
        here = at_rows(p * piece, piece)
        for side_x in range(2):

            @pl.when(xl == side_x)
            def _():
                for s in range(2 * zs):
                    dst = hp if s % 2 == side_x else ho
                    to = (s // 2) * rows
                    dst[here, to : to + rows] = hv[here, s * rows : (s + 1) * rows]

        send_heads(p).start()
        return 0

    lax.fori_loop(0, PIECES, split_heads, 0)
    own_chunk(1)
    load_res.wait()
    load_cot.wait()

    def z_step(c):
        @pl.when(c + 2 < nc)
        def _():
            own_chunk(c + 2)

        for d in range(2):
            send_own(d, c).wait_recv()
            send_on(d, c).start()

    def s_step(c):
        for d in range(2):
            send_on(d, c).wait_recv()
        sb[c] = dot(hp[tok : 2 * tok, :], wb[c]).astype(BF16)
        send_sum(c).start()
        sv[c] = dot(hp[0:tok, :], wb[c])

    def scaled(c):
        return gain[:, at_cols(c)] * cv[:, at_cols(c)].astype(F32)

    def f_step(c):
        send_sum(c).wait_recv()
        s = sv[c] + srv[c].astype(F32) + rv[:, at_cols(c)].astype(F32)
        sv[c] = s
        sq = s * s
        pr = scaled(c) * s
        a1, a2 = acc1[...], acc2[...]
        for k in range(CW // 128):
            a1 += sq[:, k * 128 : (k + 1) * 128]
            a2 += pr[:, k * 128 : (k + 1) * 128]
        acc1[...] = a1
        acc2[...] = a2

    def turn(j):
        lanes = pl.ds(pl.multiple_of(j * 128, 128), 128)
        ht[at_rows(j * 128, 128), :] = hp[:, lanes].T

    acc1[...] = jnp.zeros_like(acc1)
    acc2[...] = jnp.zeros_like(acc2)

    def lead_body(i, _):
        z_step(i)
        return 0

    lax.fori_loop(0, LEAD, lead_body, 0)
    for p in range(PIECES):
        send_heads(p).wait_recv()
    s_step(0)
    turns = kh // 128
    per = -(-turns // (nc - LEAD))

    def main_body(i, _):
        z_step(i)
        s_step(i - LEAD + 1)

        @pl.when(i >= LEAD + 2)
        def _():
            f_step(i - LEAD - 2)

        def turn_body(j, _):
            turn(j)
            return 0

        first = (i - LEAD) * per
        lax.fori_loop(first, jnp.minimum(first + per, turns), turn_body, 0)
        return 0

    lax.fori_loop(LEAD, nc, main_body, 0)

    def rest_s(c, _):
        s_step(c)
        return 0

    lax.fori_loop(nc - LEAD + 1, nc, rest_s, 0)

    def rest_f(c, _):
        f_step(c)
        return 0

    lax.fori_loop(nc - LEAD - 2, nc, rest_f, 0)

    inverse = lax.rsqrt(jnp.sum(acc1[...], axis=1, keepdims=True) / cols + EPS)
    factor = inverse * inverse * inverse * (jnp.sum(acc2[...], axis=1, keepdims=True) / cols)
    acc1[...] = jnp.broadcast_to(inverse, acc1.shape)
    acc2[...] = jnp.broadcast_to(factor, acc2.shape)

    def u_step(c, _):
        sc = scaled(c)
        for k in range(CW // 128):
            lane = slice(k * 128, (k + 1) * 128)
            ub[c, 0:tok, lane] = (acc1[...] * sc[:, lane] - sv[c, :, lane] * acc2[...]).astype(BF16)
        send_unit(c).start()
        return 0

    lax.fori_loop(0, nc, u_step, 0)
    wv[...] = jnp.full(wv.shape, 0.5 * weight, F32)
    send_weight.start()

    def d_step(c):
        def block(zd):
            at = at_rows(zd * rows, rows)
            pb[c, at, :] = dot(ht[at, :], ub[c]).astype(BF16)

        block(zo)
        for d in range(2):
            send_far(d, c).start()

        def others(j, _):
            block((z + j) % zs)
            return 0

        lax.fori_loop(0, 2, others, 0)
        block(zm)

    def b_step(c):
        for d in range(2):
            send_far(d, c).wait_recv()
            at = at_rows((zm if d else zp) * rows + d * half, half)
            pb[c, at, :] = (pb[c, at, :].astype(F32) + st1[d, c].astype(F32)).astype(BF16)
            send_near(d, c).start()

    def c_step(c):
        for d in range(2):
            send_near(d, c).wait_recv()
        total = pb[c, at_rows(z * rows, rows), :].astype(F32) + st2[0, c].astype(F32) + st2[1, c].astype(F32)
        ob[c] = (0.5 * (pv[c] - 0.004 * total)).astype(BF16)
        send_out(c).start()
        dwv[c] = total.astype(BF16)
        store_dw(c).start()

    gacc[...] = jnp.zeros_like(gacc)

    def g_step(c, _):
        send_unit(c).wait_recv()

        def part(t, _):
            at = at_rows(t * tok, tok)
            gacc[at, :] += dot_t(ub[c, at, :], wb[c])
            return 0

        lax.fori_loop(0, 2, part, 0)
        return 0

    def g_count(i):
        return jnp.minimum((5 * i + 2) // 4, nc)

    g_last = next(i for i in range(nc) if (5 * (i + 1) + 2) // 4 >= nc)

    def back_body(i, _):
        lax.fori_loop(g_count(i), g_count(i + 1), g_step, 0)

        @pl.when(i == g_last)
        def _():
            def give(p, _):
                here = at_rows(p * piece, piece)
                gsend[here, :] = gacc[at_rows(tok + p * piece, piece), :].astype(BF16)
                send_grad(p).start()
                return 0

            lax.fori_loop(0, PIECES, give, 0)
            gb[...] = gacc[0:tok, :].astype(BF16)
            store_own.start()

        d_step(i)

        @pl.when(i >= 1)
        def _():
            b_step(i - 1)

        @pl.when(i >= 2)
        def _():
            c_step(i - 2)

        return 0

    lax.fori_loop(0, nc, back_body, 0)
    b_step(nc - 1)
    c_step(nc - 2)
    c_step(nc - 1)

    def drain(c, _):
        for d in range(2):
            send_own(d, c).wait_send()
            send_on(d, c).wait_send()
            send_far(d, c).wait_send()
            send_near(d, c).wait_send()
        send_sum(c).wait_send()
        send_unit(c).wait_send()
        store_dw(c).wait()
        send_out(c).wait()
        return 0

    lax.fori_loop(0, nc, drain, 0)
    for p in range(PIECES):
        send_heads(p).wait_send()
        send_grad(p).wait()
    send_weight.wait()
    store_own.wait()


def step(by, params, push, heads, residual, cotangent, gain):
    rows, cols = params.shape
    tok = heads.shape[0]
    zs = lax.axis_size("fsdp") // 2
    nc = cols // CW
    kh = zs * rows
    half = rows // 2
    anywhere = pl.BlockSpec(memory_space=pl.ANY)
    dma = pltpu.SemaphoreType.DMA
    return pl.pallas_call(
        functools.partial(step_kernel, by, zs, heads.shape[1]),
        out_shape=(
            jax.ShapeDtypeStruct((tok, kh), BF16),
            jax.ShapeDtypeStruct((tok, kh), BF16),
            jax.ShapeDtypeStruct((rows, cols), BF16),
            jax.ShapeDtypeStruct((rows, cols), BF16),
            jax.ShapeDtypeStruct((8, 128), F32),
        ),
        in_specs=[
            anywhere,
            pl.BlockSpec(memory_space=pltpu.SMEM),
            anywhere,
            anywhere,
            anywhere,
            pl.BlockSpec(memory_space=pltpu.VMEM),
        ],
        out_specs=[anywhere] * 5,
        scratch_shapes=[
            pltpu.VMEM((nc, rows, CW), F32),
            pltpu.VMEM((tok, cols), BF16),
            pltpu.VMEM((tok, cols), BF16),
            pltpu.VMEM((tok, cols), BF16),
            pltpu.VMEM((2 * tok, kh), BF16),
            pltpu.VMEM((tok, kh), BF16),
            pltpu.VMEM((kh, 2 * tok), BF16),
            pltpu.VMEM((nc, kh, CW), BF16),
            pltpu.VMEM((nc, tok, CW), F32),
            pltpu.VMEM((nc, tok, CW), BF16),
            pltpu.VMEM((nc, tok, CW), BF16),
            pltpu.VMEM((tok, 128), F32),
            pltpu.VMEM((tok, 128), F32),
            pltpu.VMEM((nc, 2 * tok, CW), BF16),
            pltpu.VMEM((nc, kh, CW), BF16),
            pltpu.VMEM((2, nc, half, CW), BF16),
            pltpu.VMEM((2, nc, rows, CW), BF16),
            pltpu.VMEM((2 * tok, kh), F32),
            pltpu.VMEM((tok, kh), BF16),
            pltpu.VMEM((tok, kh), BF16),
            pltpu.VMEM((nc, rows, CW), BF16),
            pltpu.VMEM((nc, rows, CW), BF16),
            pltpu.VMEM((8, 128), F32),
            dma((nc,)), dma((3,)),
            dma((PIECES,)), dma((PIECES,)),
            dma((2, nc)), dma((2, nc)),
            dma((2, nc)), dma((2, nc)),
            dma((nc,)), dma((nc,)),
            dma((nc,)), dma((nc,)),
            dma((2, nc)), dma((2, nc)),
            dma((2, nc)), dma((2, nc)),
            dma((PIECES,)), dma((PIECES,)),
            dma((nc,)), dma((nc,)),
            dma((1,)), dma((1,)),
            dma((nc,)), dma((1,)),
        ],
        compiler_params=pltpu.CompilerParams(
            collective_id=by.bit_length(), has_side_effects=True, vmem_limit_bytes=62 * 2**20
        ),
        cost_estimate=pl.CostEstimate(
            flops=6 * tok * cols * heads.shape[1], bytes_accessed=20 * 2**20, transcendentals=tok
        ),
        name=f"push_sum_step_{by}",
    )(params, push, heads, residual, cotangent, gain)


def finish_kernel(zs, g_own, g_got, dw, box, params, inbox, grad, new, out):
    xl = lax.axis_index("fsdp") % 2
    width = g_own.shape[1] // zs
    for side_x in range(2):

        @pl.when(xl == side_x)
        def _():
            for s in range(2 * zs):
                src = g_own if s % 2 == side_x else g_got
                at = (s // 2) * width
                grad[:, s * width : (s + 1) * width] = src[:, at : at + width]

    new[...] = 0.5 * (params[...] - 0.004 * dw[...].astype(F32)) + inbox[...]
    out[...] = box[...].astype(F32)


def finish(g_own, g_got, dw, box, params, inbox):
    rows, cols = params.shape
    tok, kh = g_own.shape
    zs = lax.axis_size("fsdp") // 2
    steps = 4
    short = pl.BlockSpec((tok // steps, kh), lambda i: (i, 0))
    wide = pl.BlockSpec((tok // steps, 2 * kh), lambda i: (i, 0))
    block = pl.BlockSpec((rows // steps, cols), lambda i: (i, 0))
    return pl.pallas_call(
        functools.partial(finish_kernel, zs),
        grid=(steps,),
        out_shape=(
            jax.ShapeDtypeStruct((tok, 2 * kh), BF16),
            jax.ShapeDtypeStruct((rows, cols), F32),
            jax.ShapeDtypeStruct((rows, cols), F32),
        ),
        in_specs=[short, short, block, block, block, block],
        out_specs=[wide, block, block],
        compiler_params=pltpu.CompilerParams(vmem_limit_bytes=40 * 2**20),
        name="finish",
    )(g_own, g_got, dw, box, params, inbox)


def local(params, push_weight, inbox_params, inbox_weight, heads, residual, cotangent, gain, offset):
    levels = lax.axis_size("rep").bit_length() - 1
    powers = jnp.left_shift(jnp.ones((levels,), jnp.int32), jnp.arange(levels, dtype=jnp.int32))
    level = jnp.sum(jnp.where(powers == offset[0], jnp.arange(levels, dtype=jnp.int32), 0))
    operands = (params[0], push_weight, heads[0], residual[0], cotangent[0], gain[None])
    branches = [functools.partial(step, 1 << level_bit) for level_bit in range(levels)]
    g_own, g_got, dw, box, weight = lax.switch(level, branches, *operands)
    grad, new, out = finish(g_own, g_got, dw, box, params[0], inbox_params[0])
    return (new[None], 0.5 * push_weight + inbox_weight, out[None], weight[0, :1], grad[None])


def solution(mesh):
    block = P("rep", "fsdp", None)
    return jax.shard_map(
        local,
        mesh=mesh,
        in_specs=(block, P("rep"), block, P("rep"), block, block, block, P(), P()),
        out_specs=(block, P("rep"), block, P("rep"), block),
        check_vma=False,
    )
```

time: 635 us -> 165 us (0.26)
  waiting for transfers between devices: 535 us -> 0 us
  Pallas kernels: 0 us -> 156 us
  matrix products: 31.8 us -> 0 us
  local copies, waits for them, and re-layouts: 30.8 us -> 3.16 us
  between operations: 19.2 us -> 3.72 us
  other arithmetic: 11.6 us -> 1.28 us
    all_gather x1 -> x0, waiting for transfers between devices: 251 us -> none  [local(): full_weights = lax.all_gather(weights_shard, 'fsdp', axis=0, tiled=True)]
    reduce_scatter x1 -> x0, waiting for transfers between devices: 247 us -> none  [local(): lax.psum_scatter(lax.dot_general(head_rows, unit_grad, (((0,), (0,)), (()...]
    pallas_call x0 -> x2, Pallas kernels: none -> 156 us  [the longest x1 149 us: step(): pl.pallas_call(functools.partial(step_kernel, by, zs, heads.shape[1]), ou...]
    ppermute x2 -> x0, waiting for transfers between devices: 36.3 us -> none  [passed_along(): lax.ppermute(value, axis, [(i, (i + by) % length) for i in range(length)])]
    dot_general x3 -> x0, matrix products: 31.8 us -> none  [the longest x1 11.7 us: local(): jnp.dot(head_rows, full_weights, preferred_element_type=jnp.float32)]
    unnamed x18 -> x2, local copies, waits for them, and re-layouts: 30.8 us -> 1.93 us
  transfers between devices with their start and end apart: 4 -> 0, of which waited for: 3 -> 0; matrix products, arithmetic and copies ran while one was open for 3% -> 0% of each run, Pallas kernels for 0% -> 0%
where the time goes in v1:
time: 165 us
  Pallas kernels  156 us (95%)
  between operations  3.72 us (2%)
  local copies, waits for them, and re-layouts  3.16 us (2%)
    pallas_call x1, Pallas kernels, step(): pl.pallas_call(functools.partial(step_kernel, by, zs, heads.shape[1]), ou...  149 us
    pallas_call x1, Pallas kernels, finish(): pl.pallas_call(functools.partial(finish_kernel, zs), grid=(steps,), out_s...  6.96 us

profile of v1, /device:TPU:0, one launch (start us, length us, event | category | flops | bytes accessed | tf_op | source)
XLA Modules:
  0.0 164.7 jit_solution(13944105253384409383)
XLA Ops:
  1.9 1.3 fusion
  3.9 0.7 broadcast_in_dim.17
  4.6 149.6 %conditional.1 = ((bf16[384,1280]{1,0:T(8,128)(2,1)}, bf16[384,1280]{1,0:T(8,128)(2,1)}, bf16[320,2560]{1,0:T(8,128)(2,1)S(1)}, bf16[320,2560]{1,0:T(8,128)(2,1)}, f32[8,128]{1,0:T(8,128)S(1)})) conditional(s32[]{:T(128)} %clamp.3, (f32[320,2560]{1,0:T(8,128)}, f32[1]{0:T(128)}, bf16[384,2560]{1,0:T(8,128)(2,1)}, ...), branch_computations={%region_1.2_spmd, %region_2.3_spmd, %region_3.4_spmd, %region_4.5_... | conditional | flops 15099494400 | bytes 20971528 | solution.py:474
  4.6 149.4 %push_sum_step_8.1 = (bf16[384,1280]{1,0:T(8,128)(2,1)}, bf16[384,1280]{1,0:T(8,128)(2,1)}, bf16[320,2560]{1,0:T(8,128)(2,1)S(1)}, bf16[320,2560]{1,0:T(8,128)(2,1)}, f32[8,128]{1,0:T(8,128)S(1)}) custom-call(f32[320,2560]{1,0:T(8,128)} %get-tuple-element.93.params, f32[1]{0:T(128)} %get-tuple-element.94.push, bf16[384,2560]{1,0:T(8,128)(2,1)} %get-tuple-element.95.heads, ...), custom_call_target="tpu_custom_call" | custom-call | flops 15099494400 | bytes 20971520 | tf_op jit(solution)/shard_map/cond/branch_3_fun/push_sum_step_8/pallas_call | solution.py:364
  154.2 0.5 slice.17
  154.7 0.0 copy-start
  154.7 1.9 %copy-done = f32[1,320,2560]{2,1,0:T(8,128)S(1)} copy-done((f32[1,320,2560]{2,1,0:T(8,128)S(1)}, f32[1,320,2560]{2,1,0:T(8,128)}, u32[]{:S(2)}) %copy-start) | copy-done | bytes 3276824
  156.6 7.0 %finish.1 = (bf16[384,2560]{1,0:T(8,128)(2,1)}, f32[320,2560]{1,0:T(8,128)}, f32[320,2560]{1,0:T(8,128)}) custom-call(bf16[384,1280]{1,0:T(8,128)(2,1)} %get-tuple-element.146.g_own, bf16[384,1280]{1,0:T(8,128)(2,1)} %get-tuple-element.145.g_got, bf16[320,2560]{1,0:T(8,128)(2,1)S(1)} %get-tuple-element.144.dw, bf16[320,2560]{1,0:T(8,128)(2,1)} %get-tuple-element.143.box, ...), custom_call_target="tpu_custom_call" | custom-call | tf_op jit(solution)/shard_map/finish/pallas_call | solution.py:453
Async XLA Ops:
  154.7 1.9 %copy-start = (f32[1,320,2560]{2,1,0:T(8,128)S(1)}, f32[1,320,2560]{2,1,0:T(8,128)}, u32[]{:S(2)}) copy-start(f32[1,320,2560]{2,1,0:T(8,128)} %param.15) | copy-start | bytes 9830404

commit v2 on v1

v2 whole, which is shorter than its diff:
```python
import functools

import jax
import jax.numpy as jnp
from jax import lax
from jax.experimental import pallas as pl
from jax.experimental.pallas import tpu as pltpu
from jax.sharding import PartitionSpec as P

MESH = pl.DeviceIdType.MESH
F32 = jnp.float32
BF16 = jnp.bfloat16

CW = 256
LEAD = 4
EPS = 1e-05
VMEM_MB = 47


def dot(a, b):
    return jnp.dot(a, b, preferred_element_type=F32)


def dot_t(a, b):
    return lax.dot_general(a, b, (((1,), (1,)), ((), ())), preferred_element_type=F32)


def far_rows(by, rows):
    return {1: rows // 4, 2: 0}.get(by, rows // 2)


def step_kernel(
    by, inner,
    params, push, inbox, heads, residual, cotangent, gain,
    grad, new, outbox, w_out,
    pv, iv, rv, cv, gv, pw, hp, ht, wb, sv, sb, srv, acc1, acc2, ub, pb, st1, st2, wv,
    lp, lx, hs, hr, aos, aor, afs, afr, ss, sr, us, ur, s1s, s1r, s2s, s2r, gs, gr, os_, or_, ws, wr, nws, gos,
):
    rows, cols = params.shape
    tok = heads.shape[0]
    th = tok // 2
    nc = cols // CW
    kh = 4 * rows
    reps = lax.axis_size("rep")
    r = lax.axis_index("rep")
    f = lax.axis_index("fsdp")
    z, xl = f // 2, f % 2
    t = ((z + 1) // 2) % 2
    slot = (z // 2) * 2 + xl
    slots = ((z // 2) * 2 + 1 - xl, (1 - z // 2) * 2 + xl)
    far = 3 - slot
    ways = ((r, z * 2 + 1 - xl), (r, (3 - z) * 2 + xl))
    pair = (r, (z + 1 - 2 * (z % 2)) * 2 + xl)
    ahead, behind = ((r + by) % reps, f), ((r + reps - by) % reps, f)
    n0 = far_rows(by, rows)
    far_at, far_n = (0, n0), (n0, rows - n0)
    far_ways = [d for d in range(2) if far_n[d]]
    wide = 2 * rows
    mine = (t * wide, 3 * wide - t * wide)
    other = ((1 - t) * wide, 3 * wide - (1 - t) * wide)

    def remote(src, dst, send, recv, to):
        return pltpu.make_async_remote_copy(
            src_ref=src, dst_ref=dst, send_sem=send, recv_sem=recv, device_id=to, device_id_type=MESH
        )

    def at_cols(c):
        return pl.ds(pl.multiple_of(c * CW, CW), CW)

    def at_lanes(start, size):
        return pl.ds(pl.multiple_of(start, 128), size)

    def at_rows(start, size):
        return pl.ds(pl.multiple_of(start, 16), size)

    def load_params(c):
        return pltpu.make_async_copy(params.at[:, at_cols(c)], pv.at[c], lp.at[c])

    def load_heads(j):
        return pltpu.make_async_copy(
            heads.at[:, at_lanes(mine[j], wide)], hp.at[pl.ds(0, tok), pl.ds(j * wide, wide)], lx.at[j]
        )

    load_res = pltpu.make_async_copy(residual, rv, lx.at[2])
    load_cot = pltpu.make_async_copy(cotangent, cv, lx.at[3])
    load_gain = pltpu.make_async_copy(gain, gv, lx.at[4])
    load_inbox = pltpu.make_async_copy(inbox, iv, lx.at[5])
    load_push = pltpu.make_async_copy(push, pw, lx.at[6])

    def send_heads(h, j):
        return remote(
            heads.at[pl.ds(h * th, th), at_lanes(other[j], wide)],
            hp.at[pl.ds(tok + h * th, th), pl.ds(j * wide, wide)],
            hs.at[h, j], hr.at[h, j], pair,
        )

    def send_own(d, c):
        block = wb.at[c, at_rows(slot * rows, rows)]
        return remote(block, block, aos.at[d, c], aor.at[d, c], ways[d])

    def send_on(d, c):
        block = wb.at[c, at_rows(slots[1 - d] * rows + d * (rows // 2), rows // 2)]
        return remote(block, block, afs.at[d, c], afr.at[d, c], ways[d])

    def send_sum(c, h):
        return remote(sb.at[c, pl.ds(h * th, th)], srv.at[c, pl.ds(h * th, th)], ss.at[h, c], sr.at[h, c], pair)

    def send_unit(c, h):
        here, there = pl.ds(h * th, th), pl.ds(tok + h * th, th)
        return remote(ub.at[c, here], ub.at[c, there], us.at[h, c], ur.at[h, c], pair)

    def send_far(d, c):
        block = pb.at[c, at_rows(far * rows + far_at[d], far_n[d])]
        return remote(block, st1.at[c, pl.ds(far_at[d], far_n[d])], s1s.at[d, c], s1r.at[d, c], ways[d])

    def send_near(d, c):
        block = pb.at[c, at_rows(slots[d] * rows, rows)]
        return remote(block, st2.at[d, c], s2s.at[d, c], s2r.at[d, c], ways[d])

    def send_grad(h, j):
        here = pl.ds(h * th, th)
        return remote(
            hp.at[pl.ds(tok + h * th, th), pl.ds(j * wide, wide)], grad.at[here, at_lanes(mine[j], wide)],
            gs.at[h, j], gr.at[h, j], pair,
        )

    def send_out(c):
        return remote(pb.at[c, at_rows(slot * rows, rows)], outbox.at[:, at_cols(c)], os_.at[c], or_.at[c], ahead)

    send_weight = remote(wv, w_out, ws.at[0], wr.at[0], ahead)

    def store_new(c):
        return pltpu.make_async_copy(pv.at[c], new.at[:, at_cols(c)], nws.at[c])

    def store_grad(j):
        here = hp.at[pl.ds(0, tok), pl.ds(j * wide, wide)]
        return pltpu.make_async_copy(here, grad.at[:, at_lanes(mine[j], wide)], gos.at[j])

    load_push.start()
    for c in range(2):
        load_params(c).start()
    for j in range(2):
        load_heads(j).start()

    def loads(c, _):
        load_params(c).start()
        return 0

    lax.fori_loop(2, nc, loads, 0)
    load_gain.start()
    load_res.start()
    load_cot.start()
    load_inbox.start()

    barrier = pltpu.get_barrier_semaphore()
    for device in ways + (pair, ahead, behind):
        pl.semaphore_signal(barrier, inc=1, device_id=device, device_id_type=MESH)
    pl.semaphore_wait(barrier, 5)
    for h in range(2):
        for j in range(2):
            send_heads(h, j).start()

    load_push.wait()
    weight = pw[0]
    scale = (inner ** -0.5) / jnp.full((1, CW), weight, F32)

    def own_chunk(c):
        load_params(c).wait()
        wb[c, at_rows(slot * rows, rows), :] = (pv[c] * scale).astype(BF16)
        for d in range(2):
            send_own(d, c).start()

    def first_own(c, _):
        own_chunk(c)
        return 0

    lax.fori_loop(0, 2, first_own, 0)
    acc1[...] = jnp.zeros_like(acc1)
    acc2[...] = jnp.zeros_like(acc2)
    for j in range(2):
        load_heads(j).wait()
    load_gain.wait()
    load_res.wait()
    load_cot.wait()

    def z_step(c):
        @pl.when(c + 2 < nc)
        def _():
            own_chunk(c + 2)

        for d in range(2):
            send_own(d, c).wait_recv()
            send_on(1 - d, c).start()

    def s_ready(c):
        for d in range(2):
            send_on(d, c).wait_recv()

    def s_other(c, h):
        at = pl.ds(pl.multiple_of(h * th, th), th)
        sb[c, at, :] = dot(hp[pl.ds(pl.multiple_of(tok + h * th, th), th), :], wb[c]).astype(BF16)
        send_sum(c, h).start()

    def s_mine(c):
        sv[c] = dot(hp[0:tok, :], wb[c])

    def s_step(c, _):
        s_ready(c)

        def one(h, _):
            s_other(c, h)
            return 0

        lax.fori_loop(0, 2, one, 0)
        s_mine(c)
        return 0

    lanes = [slice(k * 128, (k + 1) * 128) for k in range(CW // 128)]

    def scaled(c, h):
        at = pl.ds(pl.multiple_of(h * th, th), th)
        cot = cv[at, at_cols(c)].astype(F32)
        return [gv[pl.ds(c * len(lanes) + k, 1), :] * cot[:, lane] for k, lane in enumerate(lanes)]

    def f_step(c, h):
        at = pl.ds(pl.multiple_of(h * th, th), th)
        send_sum(c, h).wait_recv()
        s = sv[c, at, :] + srv[c, at, :].astype(F32) + rv[at, at_cols(c)].astype(F32)
        sv[c, at, :] = s
        a1, a2 = acc1[at, :], acc2[at, :]
        for lane, sc in zip(lanes, scaled(c, h)):
            a1 += s[:, lane] * s[:, lane]
            a2 += sc * s[:, lane]
        acc1[at, :] = a1
        acc2[at, :] = a2

    def turn(j):
        ht[at_rows(j * 128, 128), :] = hp[:, at_lanes(j * 128, 128)].T

    def lead_body(i, _):
        z_step(i)
        return 0

    lax.fori_loop(0, LEAD - 1, lead_body, 0)
    s_ready(0)
    for h in range(2):
        for j in range(2):
            send_heads(h, j).wait_recv()
        s_other(0, h)
        if h == 0:
            z_step(LEAD - 1)
    s_mine(0)
    turns = kh // 128
    per = -(-turns // (nc - LEAD))
    twice = nc - 3

    def f_both(c, _):
        def one(h, _):
            f_step(c, h)
            return 0

        lax.fori_loop(0, 2, one, 0)
        return 0

    def main_body(i, _):
        z_step(i)
        late = (i > twice).astype(jnp.int32)
        both = (i >= twice).astype(jnp.int32)
        lax.fori_loop(i - LEAD + 1 + late, i - LEAD + 2 + both, s_step, 0)

        @pl.when(i >= LEAD + 2)
        def _():
            f_both(i - LEAD - 2, 0)

        def turn_body(j, _):
            turn(j)
            return 0

        first = (i - LEAD) * per
        lax.fori_loop(first, jnp.minimum(first + per, turns), turn_body, 0)
        return 0

    lax.fori_loop(LEAD, nc, main_body, 0)

    def last_sums(h, _):
        def one(c, _):
            @pl.when(h == 0)
            def _():
                s_ready(c)

            s_other(c, h)
            return 0

        lax.fori_loop(nc - 2, nc, one, 0)
        return 0

    lax.fori_loop(0, 2, last_sums, 0)
    for c in range(nc - 2, nc):
        s_mine(c)
    lax.fori_loop(nc - LEAD - 2, nc - 2, f_both, 0)

    def unit(c, h):
        at = pl.ds(pl.multiple_of(h * th, th), th)
        for lane, sc in zip(lanes, scaled(c, h)):
            ub[c, at, lane] = (acc1[at, :] * sc - sv[c, at, lane] * acc2[at, :]).astype(BF16)
        send_unit(c, h).start()

    def first_units(h, _):
        at = pl.ds(pl.multiple_of(h * th, th), th)

        def last_f(c, _):
            f_step(c, h)
            return 0

        lax.fori_loop(nc - 2, nc, last_f, 0)
        inverse = lax.rsqrt(jnp.sum(acc1[at, :], axis=1, keepdims=True) / cols + EPS)
        factor = inverse * inverse * inverse * (jnp.sum(acc2[at, :], axis=1, keepdims=True) / cols)
        acc1[at, :] = jnp.broadcast_to(inverse, (th, 128))
        acc2[at, :] = jnp.broadcast_to(factor, (th, 128))

        unit(0, h)
        return 0

    lax.fori_loop(0, 2, first_units, 0)

    def mid_units(c, _):
        def one(h, _):
            unit(c, h)
            return 0

        lax.fori_loop(0, 2, one, 0)
        return 0

    lax.fori_loop(1, nc - 2, mid_units, 0)

    def last_units(h, _):
        def one(c, _):
            unit(c, h)
            return 0

        lax.fori_loop(nc - 2, nc, one, 0)
        return 0

    lax.fori_loop(0, 2, last_units, 0)
    wv[...] = jnp.full(wv.shape, 0.5 * weight, F32)
    send_weight.start()
    load_inbox.wait()

    blocks = kh // CW

    def clear(k, _):
        sv[k] = jnp.zeros(sv.shape[1:], F32)
        return 0

    lax.fori_loop(0, 2 * blocks, clear, 0)

    def g_part(c, who, start, size):
        at = pl.ds(pl.multiple_of(start, th), size)
        part = dot_t(ub[c, pl.ds(pl.multiple_of(who * tok + start, th), size), :], wb[c])
        for k in range(blocks):
            sv[who * blocks + k, at, :] += part[:, k * CW : (k + 1) * CW]

    def g_half(c, h):
        send_unit(c, h).wait_recv()
        g_part(c, 1, h * th, th)

    def g_step(c, _):
        def one(h, _):
            g_half(c, h)
            return 0

        lax.fori_loop(0, 2, one, 0)
        g_part(c, 0, 0, tok)
        return 0

    def g_out(who, start, size):
        for k in range(blocks):
            part = sv[who * blocks + k, pl.ds(start, size), :].astype(BF16)
            hp[pl.ds(who * tok + start, size), k * CW : (k + 1) * CW] = part

    def g_last(h):
        for c in range(nc - 2, nc):
            g_half(c, h)
        g_out(1, h * th, th)
        for j in range(2):
            send_grad(h, j).start()

    def g_mine():
        for c in range(nc - 2, nc):
            g_part(c, 0, 0, tok)
        g_out(0, 0, tok)
        for j in range(2):
            store_grad(j).start()

    def g_count(i):
        return jnp.minimum(i + 1 + (i >= 3).astype(jnp.int32), nc - 2)

    def d_step(c):
        def block(s):
            at = at_rows(s * rows, rows)
            pb[c, at, :] = dot(ht[at, :], ub[c]).astype(BF16)

        block(far)
        for d in far_ways:
            send_far(d, c).start()

        def others(k, _):
            block((far + k) % 4)
            return 0

        lax.fori_loop(1, 4, others, 0)

    def b_step(c):
        for d in range(2):
            if d in far_ways:
                send_far(d, c).wait_recv()
                at = at_rows(slots[1 - d] * rows + far_at[d], far_n[d])
                got = st1[c, pl.ds(far_at[d], far_n[d]), :]
                pb[c, at, :] = (pb[c, at, :].astype(F32) + got.astype(F32)).astype(BF16)
            send_near(1 - d, c).start()

    def c_step(c):
        for d in range(2):
            send_near(d, c).wait_recv()
        total = pb[c, at_rows(slot * rows, rows), :].astype(F32) + st2[0, c].astype(F32) + st2[1, c].astype(F32)
        kept = 0.5 * (pv[c] - 0.004 * total)
        pb[c, at_rows(slot * rows, rows), :] = kept.astype(BF16)
        send_out(c).start()
        pv[c] = kept + iv[:, at_cols(c)]
        store_new(c).start()

    def back_body(i, _):
        before = jnp.where(i == 0, 0, g_count(i - 1))
        lax.fori_loop(before, g_count(i), g_step, 0)

        d_step(i)

        @pl.when(i >= 1)
        def _():
            b_step(i - 1)

        @pl.when(i == nc - 4)
        def _():
            g_last(0)

        @pl.when(i == nc - 3)
        def _():
            g_last(1)

        @pl.when(i >= 2)
        def _():
            c_step(i - 2)

        @pl.when(i == nc - 2)
        def _():
            g_mine()

        for d in range(2):
            send_own(d, i).wait_send()
            send_on(d, i).wait_send()
            send_sum(i, d).wait_send()
            send_unit(i, d).wait_send()
        return 0

    lax.fori_loop(0, nc, back_body, 0)
    b_step(nc - 1)
    c_step(nc - 2)
    c_step(nc - 1)

    def drain(c, _):
        for d in range(2):
            if d in far_ways:
                send_far(d, c).wait_send()
            send_near(d, c).wait_send()
        store_new(c).wait()
        send_out(c).wait()
        return 0

    lax.fori_loop(0, nc, drain, 0)
    for h in range(2):
        for j in range(2):
            send_heads(h, j).wait_send()
            send_grad(h, j).wait()
        store_grad(h).wait()
    send_weight.wait()


def step(by, params, push, inbox, heads, residual, cotangent, gain):
    rows, cols = params.shape
    tok = heads.shape[0]
    nc = cols // CW
    kh = 4 * rows
    anywhere = pl.BlockSpec(memory_space=pl.ANY)
    dma = pltpu.SemaphoreType.DMA
    return pl.pallas_call(
        functools.partial(step_kernel, by, heads.shape[1]),
        out_shape=(
            pltpu.VMEM(heads.shape, BF16),
            pltpu.VMEM((rows, cols), F32),
            pltpu.VMEM((rows, cols), BF16),
            pltpu.VMEM((8, 128), F32),
        ),
        in_specs=[pl.BlockSpec(memory_space=pltpu.HBM)] * 7,
        out_specs=[anywhere] * 4,
        scratch_shapes=[
            pltpu.VMEM((nc, rows, CW), F32),
            pltpu.VMEM((rows, cols), F32),
            pltpu.VMEM((tok, cols), BF16),
            pltpu.VMEM((tok, cols), BF16),
            pltpu.VMEM(gain.shape, F32),
            pltpu.SMEM((1,), F32),
            pltpu.VMEM((2 * tok, kh), BF16),
            pltpu.VMEM((kh, 2 * tok), BF16),
            pltpu.VMEM((nc, kh, CW), BF16),
            pltpu.VMEM((nc, tok, CW), F32),
            pltpu.VMEM((nc, tok, CW), BF16),
            pltpu.VMEM((nc, tok, CW), BF16),
            pltpu.VMEM((tok, 128), F32),
            pltpu.VMEM((tok, 128), F32),
            pltpu.VMEM((nc, 2 * tok, CW), BF16),
            pltpu.VMEM((nc, kh, CW), BF16),
            pltpu.VMEM((nc, rows, CW), BF16),
            pltpu.VMEM((2, nc, rows, CW), BF16),
            pltpu.VMEM((8, 128), F32),
            dma((nc,)), dma((7,)),
            dma((2, 2)), dma((2, 2)),
            dma((2, nc)), dma((2, nc)),
            dma((2, nc)), dma((2, nc)),
            dma((2, nc)), dma((2, nc)),
            dma((2, nc)), dma((2, nc)),
            dma((2, nc)), dma((2, nc)),
            dma((2, nc)), dma((2, nc)),
            dma((2, 2)), dma((2, 2)),
            dma((nc,)), dma((nc,)),
            dma((1,)), dma((1,)),
            dma((nc,)), dma((2,)),
        ],
        compiler_params=pltpu.CompilerParams(
            collective_id=by.bit_length(), has_side_effects=True, vmem_limit_bytes=VMEM_MB * 2**20
        ),
        cost_estimate=pl.CostEstimate(
            flops=6 * tok * cols * heads.shape[1], bytes_accessed=20 * 2**20, transcendentals=tok
        ),
        name=f"push_sum_step_{by}",
    )(params, push, inbox, heads, residual, cotangent, gain)


def finish_kernel(g_in, n_in, box, w_in, push, inbox, grad, new, out, w_out, w_new, ov, pw, iw, ww, sem, csem):
    ww[0] = w_in[0, 0]
    steps = sem.shape[0]
    size = box.shape[0] // steps
    copies = [
        pltpu.make_async_copy(push, pw, csem.at[0]),
        pltpu.make_async_copy(inbox, iw, csem.at[1]),
        pltpu.make_async_copy(n_in, new, csem.at[2]),
        pltpu.make_async_copy(g_in, grad, csem.at[3]),
        pltpu.make_async_copy(ww, w_out, csem.at[4]),
    ]
    for copy in copies:
        copy.start()
    for k in range(steps):
        at = pl.ds(k * size, size)
        ov[at, :] = box[at, :].astype(F32)
        copies.append(pltpu.make_async_copy(ov.at[at], out.at[at], sem.at[k]))
        copies[-1].start()
        if k == 0:
            copies[0].wait()
            copies[1].wait()
            pw[0] = 0.5 * pw[0] + iw[0]
            copies.append(pltpu.make_async_copy(pw, w_new, csem.at[5]))
            copies[-1].start()
    for copy in copies[2:]:
        copy.wait()


def finish(g_in, n_in, box, w_in, push, inbox):
    rows, cols = box.shape
    anywhere = pl.BlockSpec(memory_space=pl.ANY)
    steps = 4
    return pl.pallas_call(
        finish_kernel,
        out_shape=(
            jax.ShapeDtypeStruct(g_in.shape, BF16),
            jax.ShapeDtypeStruct((rows, cols), F32),
            jax.ShapeDtypeStruct((rows, cols), F32),
            jax.ShapeDtypeStruct((1,), F32),
            jax.ShapeDtypeStruct((1,), F32),
        ),
        in_specs=[pl.BlockSpec(memory_space=pltpu.VMEM)] * 4 + [pl.BlockSpec(memory_space=pltpu.HBM)] * 2,
        out_specs=[anywhere] * 5,
        scratch_shapes=[
            pltpu.VMEM((rows, cols), F32),
            pltpu.SMEM((1,), F32),
            pltpu.SMEM((1,), F32),
            pltpu.SMEM((1,), F32),
            pltpu.SemaphoreType.DMA((steps,)),
            pltpu.SemaphoreType.DMA((6,)),
        ],
        compiler_params=pltpu.CompilerParams(vmem_limit_bytes=16 * 2**20),
        name="finish",
    )(g_in, n_in, box, w_in, push, inbox)


def whole(by, params, push, inbox, inbox_weight, heads, residual, cotangent, gain):
    g, new, box, weight = step(by, params, push, inbox, heads, residual, cotangent, gain)
    return finish(g, new, box, weight, push, inbox_weight)


def local(params, push_weight, inbox_params, inbox_weight, heads, residual, cotangent, gain, offset):
    operands = (
        params[0], push_weight, inbox_params[0], inbox_weight, heads[0], residual[0], cotangent[0], gain.reshape(-1, 128)
    )
    branches = [functools.partial(whole, 1 << bit) for bit in range(4)]
    grad, new, out, weight, new_weight = lax.switch(offset[0] >> 1, branches, *operands)
    return (new[None], new_weight, out[None], weight, grad[None])


def solution(mesh):
    block = P("rep", "fsdp", None)
    return jax.shard_map(
        local,
        mesh=mesh,
        in_specs=(block, P("rep"), block, P("rep"), block, block, block, P(), P()),
        out_specs=(block, P("rep"), block, P("rep"), block),
        check_vma=False,
    )
```

time: 165 us -> 152 us (0.921)
  Pallas kernels: 156 us -> 149 us
  local copies, waits for them, and re-layouts: 3.16 us -> 0 us
  between operations: 3.72 us -> 1.5 us
    pallas_call x2, Pallas kernels: 156 us -> 149 us  [the longest x1 145 us: step(): pl.pallas_call(functools.partial(step_kernel, by, heads.shape[1]), out_sh...]
    unnamed x2 -> x0, local copies, waits for them, and re-layouts: 1.93 us -> none
where the time goes in v2:
time: 152 us
  Pallas kernels  149 us (98%)
    pallas_call x1, Pallas kernels, step(): pl.pallas_call(functools.partial(step_kernel, by, heads.shape[1]), out_sh...  145 us
    pallas_call x1, Pallas kernels, finish(): pl.pallas_call(finish_kernel, out_shape=(jax.ShapeDtypeStruct(g_in.shape,...  4.74 us

profile of v2, /device:TPU:0, one launch (start us, length us, event | category | flops | bytes accessed | tf_op | source)
XLA Modules:
  0.0 151.8 jit_solution(3359523260943390582)
XLA Ops:
  1.3 150.3 %conditional.1 = ((bf16[384,2560]{1,0:T(8,128)(2,1)}, f32[320,2560]{1,0:T(8,128)}, f32[320,2560]{1,0:T(8,128)}, f32[1]{0:T(128)}, f32[1]{0:T(128)})) conditional(s32[]{:T(128)} %bitcast, (f32[320,2560]{1,0:T(8,128)}, f32[1]{0:T(128)}, f32[320,2560]{1,0:T(8,128)}, bf16[384,2560]{1,0:T(8,128)(2,1)}, ...), branch_computations={%region_0.0_spmd.clone, %region_1.0_spmd.clone, %region_2.0_spmd.c... | conditional | flops 15099494400 | bytes 20971528 | solution.py:614
  1.8 144.7 %push_sum_step_8.2 = (bf16[384,2560]{1,0:T(8,128)(2,1)S(1)}, f32[320,2560]{1,0:T(8,128)S(1)}, bf16[320,2560]{1,0:T(8,128)(2,1)S(1)}, f32[8,128]{1,0:T(8,128)S(1)}) custom-call(f32[320,2560]{1,0:T(8,128)} %get-tuple-element.230.params, f32[1]{0:T(128)} %get-tuple-element.231.push, f32[320,2560]{1,0:T(8,128)} %get-tuple-element.232.inbox, ...), custom_call_target="tpu_custom_call" | custom-call | flops 15099494400 | bytes 20971520 | tf_op jit(solution)/shard_map/cond/branch_3_fun/push_sum_step_8/pallas_call | solution.py:495
  146.5 4.7 %finish.11 = (bf16[384,2560]{1,0:T(8,128)(2,1)}, f32[320,2560]{1,0:T(8,128)}, f32[320,2560]{1,0:T(8,128)}, f32[1]{0:T(128)}, f32[1]{0:T(128)}) custom-call(bf16[384,2560]{1,0:T(8,128)(2,1)S(1)} %get-tuple-element.237.g_in, f32[320,2560]{1,0:T(8,128)S(1)} %get-tuple-element.238.n_in, bf16[320,2560]{1,0:T(8,128)(2,1)S(1)} %get-tuple-element.239.box, ...), custom_call_target="tpu_custom_call" | custom-call | tf_op jit(solution)/shard_map/cond/branch_3_fun/finish/pallas_call | solution.py:580

commit v3 on v2

--- a/solution.py
+++ b/solution.py
@@ -12,9 +12,11 @@
 BF16 = jnp.bfloat16
 
 CW = 256
+CF1, CF2 = 6, 2
 LEAD = 4
+AHEAD = 3
 EPS = 1e-05
-VMEM_MB = 47
+VMEM_MB = 51
 
 
 def dot(a, b):
@@ -25,15 +27,23 @@
     return lax.dot_general(a, b, (((1,), (1,)), ((), ())), preferred_element_type=F32)
 
 
-def far_rows(by, rows):
-    return {1: rows // 4, 2: 0}.get(by, rows // 2)
+def loop(low, high, body):
+    def run(i, _):
+        body(i)
+        return 0
+
+    lax.fori_loop(low, high, run, 0)
+
+
+def far_by_x(by, nc):
+    return {1: CF1, 2: CF2}.get(by, nc)
 
 
 def step_kernel(
     by, inner,
     params, push, inbox, heads, residual, cotangent, gain,
     grad, new, outbox, w_out,
-    pv, iv, rv, cv, gv, pw, hp, ht, wb, sv, sb, srv, acc1, acc2, ub, pb, st1, st2, wv,
+    pv, iv, rv, cv, gv, pw, hp, ht, wb, sv, sb, srv, acc1, acc2, ub, pb, st1, st2, ga, wv,
     lp, lx, hs, hr, aos, aor, afs, afr, ss, sr, us, ur, s1s, s1r, s2s, s2r, gs, gr, os_, or_, ws, wr, nws, gos,
 ):
     rows, cols = params.shape
@@ -52,9 +62,8 @@
     ways = ((r, z * 2 + 1 - xl), (r, (3 - z) * 2 + xl))
     pair = (r, (z + 1 - 2 * (z % 2)) * 2 + xl)
     ahead, behind = ((r + by) % reps, f), ((r + reps - by) % reps, f)
-    n0 = far_rows(by, rows)
-    far_at, far_n = (0, n0), (n0, rows - n0)
-    far_ways = [d for d in range(2) if far_n[d]]
+    by_x = far_by_x(by, nc)
+    half = rows // 2
     wide = 2 * rows
     mine = (t * wide, 3 * wide - t * wide)
     other = ((1 - t) * wide, 3 * wide - (1 - t) * wide)
@@ -109,9 +118,11 @@
         here, there = pl.ds(h * th, th), pl.ds(tok + h * th, th)
         return remote(ub.at[c, here], ub.at[c, there], us.at[h, c], ur.at[h, c], pair)
 
-    def send_far(d, c):
-        block = pb.at[c, at_rows(far * rows + far_at[d], far_n[d])]
-        return remote(block, st1.at[c, pl.ds(far_at[d], far_n[d])], s1s.at[d, c], s1r.at[d, c], ways[d])
+    def send_far(k, c):
+        block = pb.at[c, at_rows(far * rows + k * half, half)]
+        x_first = (c < by_x) & (k == 0)
+        to = (r, jnp.where(x_first, ways[0][1], ways[1][1]))
+        return remote(block, st1.at[c, pl.ds(k * half, half)], s1s.at[k, c], s1r.at[k, c], to)
 
     def send_near(d, c):
         block = pb.at[c, at_rows(slots[d] * rows, rows)]
@@ -142,11 +153,7 @@
     for j in range(2):
         load_heads(j).start()
 
-    def loads(c, _):
-        load_params(c).start()
-        return 0
-
-    lax.fori_loop(2, nc, loads, 0)
+    loop(2, nc, lambda c: load_params(c).start())
     load_gain.start()
     load_res.start()
     load_cot.start()
@@ -170,11 +177,7 @@
         for d in range(2):
             send_own(d, c).start()
 
-    def first_own(c, _):
-        own_chunk(c)
-        return 0
-
-    lax.fori_loop(0, 2, first_own, 0)
+    loop(0, 2, own_chunk)
     acc1[...] = jnp.zeros_like(acc1)
     acc2[...] = jnp.zeros_like(acc2)
     for j in range(2):
@@ -204,16 +207,10 @@
     def s_mine(c):
         sv[c] = dot(hp[0:tok, :], wb[c])
 
-    def s_step(c, _):
+    def s_step(c):
         s_ready(c)
-
-        def one(h, _):
-            s_other(c, h)
-            return 0
-
-        lax.fori_loop(0, 2, one, 0)
-        s_mine(c)
-        return 0
+        loop(0, 2, lambda h: s_other(c, h))
+        s_mine(c - 1)
 
     lanes = [slice(k * 128, (k + 1) * 128) for k in range(CW // 128)]
 
@@ -237,67 +234,65 @@
     def turn(j):
         ht[at_rows(j * 128, 128), :] = hp[:, at_lanes(j * 128, 128)].T
 
-    def lead_body(i, _):
-        z_step(i)
-        return 0
-
-    lax.fori_loop(0, LEAD - 1, lead_body, 0)
-    s_ready(0)
-    for h in range(2):
+    def heads_in(h):
         for j in range(2):
             send_heads(h, j).wait_recv()
-        s_other(0, h)
-        if h == 0:
-            z_step(LEAD - 1)
-    s_mine(0)
+
+    def f_both(c):
+        loop(0, 2, lambda h: f_step(c, h))
+
+    loop(0, LEAD - 1, z_step)
+    s_ready(0)
     turns = kh // 128
     per = -(-turns // (nc - LEAD))
     twice = nc - 3
 
-    def f_both(c, _):
-        def one(h, _):
-            f_step(c, h)
-            return 0
-
-        lax.fori_loop(0, 2, one, 0)
-        return 0
-
-    def main_body(i, _):
+    def main_body(i):
+        @pl.when(i == LEAD - 1)
+        def _():
+            heads_in(0)
+            s_other(0, 0)
+
         z_step(i)
-        late = (i > twice).astype(jnp.int32)
-        both = (i >= twice).astype(jnp.int32)
-        lax.fori_loop(i - LEAD + 1 + late, i - LEAD + 2 + both, s_step, 0)
-
-        @pl.when(i >= LEAD + 2)
-        def _():
-            f_both(i - LEAD - 2, 0)
-
-        def turn_body(j, _):
-            turn(j)
-            return 0
-
-        first = (i - LEAD) * per
-        lax.fori_loop(first, jnp.minimum(first + per, turns), turn_body, 0)
-        return 0
-
-    lax.fori_loop(LEAD, nc, main_body, 0)
-
-    def last_sums(h, _):
-        def one(c, _):
+
+        @pl.when(i == LEAD - 1)
+        def _():
+            heads_in(1)
+            s_other(0, 1)
+
+        @pl.when(i >= LEAD)
+        def _():
+            late = (i > twice).astype(jnp.int32)
+            both = (i >= twice).astype(jnp.int32)
+            loop(i - LEAD + 1 + late, i - LEAD + 2 + both, s_step)
+
+            @pl.when(i >= LEAD + 2)
+            def _():
+                f_both(i - LEAD - 2)
+
+            first = (i - LEAD) * per
+            loop(first, jnp.minimum(first + per, turns), turn)
+
+    blocks = kh // CW
+
+    def clear(k):
+        ga[k] = jnp.zeros(ga.shape[1:], F32)
+
+    loop(0, 2 * blocks, clear)
+    loop(LEAD - 1, nc, main_body)
+
+    def last_sums(h):
+        def one(c):
             @pl.when(h == 0)
             def _():
                 s_ready(c)
 
             s_other(c, h)
-            return 0
-
-        lax.fori_loop(nc - 2, nc, one, 0)
-        return 0
-
-    lax.fori_loop(0, 2, last_sums, 0)
-    for c in range(nc - 2, nc):
-        s_mine(c)
-    lax.fori_loop(nc - LEAD - 2, nc - 2, f_both, 0)
+
+        loop(nc - 2, nc, one)
+
+    loop(0, 2, last_sums)
+    loop(nc - 3, nc, s_mine)
 
     def unit(c, h):
         at = pl.ds(pl.multiple_of(h * th, th), th)
@@ -305,119 +300,81 @@
             ub[c, at, lane] = (acc1[at, :] * sc - sv[c, at, lane] * acc2[at, :]).astype(BF16)
         send_unit(c, h).start()
 
-    def first_units(h, _):
+    def first_units(h):
         at = pl.ds(pl.multiple_of(h * th, th), th)
 
-        def last_f(c, _):
-            f_step(c, h)
-            return 0
-
-        lax.fori_loop(nc - 2, nc, last_f, 0)
+        loop((nc - LEAD - 2) * 2 * (1 - h), (nc - 2) * 2 * (1 - h), lambda k: f_step(k // 2, k % 2))
+        loop(nc - 2, nc, lambda c: f_step(c, h))
         inverse = lax.rsqrt(jnp.sum(acc1[at, :], axis=1, keepdims=True) / cols + EPS)
         factor = inverse * inverse * inverse * (jnp.sum(acc2[at, :], axis=1, keepdims=True) / cols)
         acc1[at, :] = jnp.broadcast_to(inverse, (th, 128))
         acc2[at, :] = jnp.broadcast_to(factor, (th, 128))
-
         unit(0, h)
-        return 0
-
-    lax.fori_loop(0, 2, first_units, 0)
-
-    def mid_units(c, _):
-        def one(h, _):
-            unit(c, h)
-            return 0
-
-        lax.fori_loop(0, 2, one, 0)
-        return 0
-
-    lax.fori_loop(1, nc - 2, mid_units, 0)
-
-    def last_units(h, _):
-        def one(c, _):
-            unit(c, h)
-            return 0
-
-        lax.fori_loop(nc - 2, nc, one, 0)
-        return 0
-
-    lax.fori_loop(0, 2, last_units, 0)
+
+    loop(0, 2, first_units)
+
+    def units(k):
+        c, h = k // 2, k % 2
+        tail = (c >= nc - 2).astype(jnp.int32)
+        j = k - 2 * (nc - 2)
+        unit(c + tail * (nc - 2 + j % 2 - c), h + tail * (j // 2 - h))
+
+    loop(2, 2 * AHEAD, units)
     wv[...] = jnp.full(wv.shape, 0.5 * weight, F32)
     send_weight.start()
     load_inbox.wait()
 
-    blocks = kh // CW
-
-    def clear(k, _):
-        sv[k] = jnp.zeros(sv.shape[1:], F32)
-        return 0
-
-    lax.fori_loop(0, 2 * blocks, clear, 0)
-
     def g_part(c, who, start, size):
         at = pl.ds(pl.multiple_of(start, th), size)
-        part = dot_t(ub[c, pl.ds(pl.multiple_of(who * tok + start, th), size), :], wb[c])
+        add = dot_t(ub[c, pl.ds(pl.multiple_of(who * tok + start, th), size), :], wb[c])
         for k in range(blocks):
-            sv[who * blocks + k, at, :] += part[:, k * CW : (k + 1) * CW]
-
-    def g_half(c, h):
-        send_unit(c, h).wait_recv()
-        g_part(c, 1, h * th, th)
-
-    def g_step(c, _):
-        def one(h, _):
-            g_half(c, h)
-            return 0
-
-        lax.fori_loop(0, 2, one, 0)
-        g_part(c, 0, 0, tok)
-        return 0
+            ga[who * blocks + k, at, :] += add[:, k * CW : (k + 1) * CW]
 
     def g_out(who, start, size):
+        at, to = pl.ds(pl.multiple_of(start, th), size), pl.ds(pl.multiple_of(who * tok + start, th), size)
         for k in range(blocks):
-            part = sv[who * blocks + k, pl.ds(start, size), :].astype(BF16)
-            hp[pl.ds(who * tok + start, size), k * CW : (k + 1) * CW] = part
+            hp[to, k * CW : (k + 1) * CW] = ga[who * blocks + k, at, :].astype(BF16)
+
+    def g_count(i):
+        return jnp.minimum(i + 1 + (i >= 3).astype(jnp.int32), nc - 2)
+
+    def u_wait(c):
+        for h in range(2):
+            send_unit(c, h).wait_recv()
 
     def g_last(h):
-        for c in range(nc - 2, nc):
-            g_half(c, h)
+        def one(c):
+            send_unit(c, h).wait_recv()
+            g_part(c, 1, h * th, th)
+
+        loop(nc - 2, nc, one)
         g_out(1, h * th, th)
         for j in range(2):
             send_grad(h, j).start()
-
-    def g_mine():
-        for c in range(nc - 2, nc):
-            g_part(c, 0, 0, tok)
-        g_out(0, 0, tok)
-        for j in range(2):
-            store_grad(j).start()
-
-    def g_count(i):
-        return jnp.minimum(i + 1 + (i >= 3).astype(jnp.int32), nc - 2)
 
     def d_step(c):
         def block(s):
             at = at_rows(s * rows, rows)
             pb[c, at, :] = dot(ht[at, :], ub[c]).astype(BF16)
 
-        block(far)
-        for d in far_ways:
-            send_far(d, c).start()
-
-        def others(k, _):
+        def one(k):
             block((far + k) % 4)
-            return 0
-
-        lax.fori_loop(1, 4, others, 0)
+
+            @pl.when(k == 0)
+            def _():
+                for d in range(2):
+                    send_far(d, c).start()
+
+        loop(0, 4, one)
 
     def b_step(c):
+        for k in range(2):
+            send_far(k, c).wait_recv()
+            x_first = (c < by_x) & (k == 0)
+            at = at_rows(jnp.where(x_first, slots[1], slots[0]) * rows + k * half, half)
+            pb[c, at, :] = (pb[c, at, :].astype(F32) + st1[c, k * half : (k + 1) * half, :].astype(F32)).astype(BF16)
         for d in range(2):
-            if d in far_ways:
-                send_far(d, c).wait_recv()
-                at = at_rows(slots[1 - d] * rows + far_at[d], far_n[d])
-                got = st1[c, pl.ds(far_at[d], far_n[d]), :]
-                pb[c, at, :] = (pb[c, at, :].astype(F32) + got.astype(F32)).astype(BF16)
-            send_near(1 - d, c).start()
+            send_near(d, c).start()
 
     def c_step(c):
         for d in range(2):
@@ -429,23 +386,28 @@
         pv[c] = kept + iv[:, at_cols(c)]
         store_new(c).start()
 
-    def back_body(i, _):
-        before = jnp.where(i == 0, 0, g_count(i - 1))
-        lax.fori_loop(before, g_count(i), g_step, 0)
-
-        d_step(i)
-
-        @pl.when(i >= 1)
+    def back_body(i):
+        before, now = jnp.where(i == 0, 0, g_count(i - 1)), g_count(i)
+        loop(before, now, u_wait)
+
+        @pl.when(i < nc)
+        def _():
+            d_step(i)
+
+        @pl.when((i >= 1) & (i <= nc))
         def _():
             b_step(i - 1)
 
-        @pl.when(i == nc - 4)
-        def _():
-            g_last(0)
-
-        @pl.when(i == nc - 3)
-        def _():
-            g_last(1)
+        loop(jnp.minimum(2 * (AHEAD + 2 * i), 2 * nc), jnp.minimum(2 * (AHEAD + 2 * i + 2), 2 * nc), units)
+
+        mine = (i == nc - 2).astype(jnp.int32)
+        loop(
+            before, now + 2 * mine, lambda c: loop(0, 2 - mine, lambda who: g_part(c, who, 0, tok))
+        )
+
+        @pl.when((i == nc - 4) | (i == nc - 3))
+        def _():
+            g_last(i - nc + 4)
 
         @pl.when(i >= 2)
         def _():
@@ -453,30 +415,28 @@
 
         @pl.when(i == nc - 2)
         def _():
-            g_mine()
-
+            g_out(0, 0, tok)
+            for j in range(2):
+                store_grad(j).start()
+
+        @pl.when(i < nc)
+        def _():
+            for d in range(2):
+                send_own(d, i).wait_send()
+                send_on(d, i).wait_send()
+                send_sum(i, d).wait_send()
+                send_unit(i, d).wait_send()
+
+    loop(0, nc + 2, back_body)
+
+    def drain(c):
         for d in range(2):
-            send_own(d, i).wait_send()
-            send_on(d, i).wait_send()
-            send_sum(i, d).wait_send()
-            send_unit(i, d).wait_send()
-        return 0
-
-    lax.fori_loop(0, nc, back_body, 0)
-    b_step(nc - 1)
-    c_step(nc - 2)
-    c_step(nc - 1)
-
-    def drain(c, _):
-        for d in range(2):
-            if d in far_ways:
-                send_far(d, c).wait_send()
+            send_far(d, c).wait_send()
             send_near(d, c).wait_send()
         store_new(c).wait()
         send_out(c).wait()
-        return 0
-
-    lax.fori_loop(0, nc, drain, 0)
+
+    loop(0, nc, drain)
     for h in range(2):
         for j in range(2):
             send_heads(h, j).wait_send()
@@ -521,6 +481,7 @@
             pltpu.VMEM((nc, kh, CW), BF16),
             pltpu.VMEM((nc, rows, CW), BF16),
             pltpu.VMEM((2, nc, rows, CW), BF16),
+            pltpu.VMEM((2 * kh // CW, tok, CW), F32),
             pltpu.VMEM((8, 128), F32),
             dma((nc,)), dma((7,)),
             dma((2, 2)), dma((2, 2)),

time: 152 us -> 150 us (0.987)
  no operation moved by 1% of the time
where the time goes in v3:
time: 150 us
  Pallas kernels  148 us (99%)
    pallas_call x1, Pallas kernels, step(): pl.pallas_call(functools.partial(step_kernel, by, heads.shape[1]), out_sh...  144 us
    pallas_call x1, Pallas kernels, finish(): pl.pallas_call(finish_kernel, out_shape=(jax.ShapeDtypeStruct(g_in.shape,...  4.74 us

profile of v3, /device:TPU:0, one launch (start us, length us, event | category | flops | bytes accessed | tf_op | source)
XLA Modules:
  0.0 150.1 jit_solution(16511467489978367935)
XLA Ops:
  1.3 148.7 %conditional.1 = ((bf16[384,2560]{1,0:T(8,128)(2,1)}, f32[320,2560]{1,0:T(8,128)}, f32[320,2560]{1,0:T(8,128)}, f32[1]{0:T(128)}, f32[1]{0:T(128)})) conditional(s32[]{:T(128)} %bitcast, (f32[320,2560]{1,0:T(8,128)}, f32[1]{0:T(128)}, f32[320,2560]{1,0:T(8,128)}, bf16[384,2560]{1,0:T(8,128)(2,1)}, ...), branch_computations={%region_0.0_spmd.clone, %region_1.0_spmd.clone, %region_2.0_spmd.c... | conditional | flops 15099494400 | bytes 20971528 | solution.py:575
  1.5 143.5 %push_sum_step_8.2 = (bf16[384,2560]{1,0:T(8,128)(2,1)S(1)}, f32[320,2560]{1,0:T(8,128)S(1)}, bf16[320,2560]{1,0:T(8,128)(2,1)S(1)}, f32[8,128]{1,0:T(8,128)S(1)}) custom-call(f32[320,2560]{1,0:T(8,128)} %get-tuple-element.230.params, f32[1]{0:T(128)} %get-tuple-element.231.push, f32[320,2560]{1,0:T(8,128)} %get-tuple-element.232.inbox, ...), custom_call_target="tpu_custom_call" | custom-call | flops 15099494400 | bytes 20971520 | tf_op jit(solution)/shard_map/cond/branch_3_fun/push_sum_step_8/pallas_call | solution.py:455
  145.0 4.7 %finish.11 = (bf16[384,2560]{1,0:T(8,128)(2,1)}, f32[320,2560]{1,0:T(8,128)}, f32[320,2560]{1,0:T(8,128)}, f32[1]{0:T(128)}, f32[1]{0:T(128)}) custom-call(bf16[384,2560]{1,0:T(8,128)(2,1)S(1)} %get-tuple-element.237.g_in, f32[320,2560]{1,0:T(8,128)S(1)} %get-tuple-element.238.n_in, bf16[320,2560]{1,0:T(8,128)(2,1)S(1)} %get-tuple-element.239.box, ...), custom_call_target="tpu_custom_call" | custom-call | tf_op jit(solution)/shard_map/cond/branch_3_fun/finish/pallas_call | solution.py:541
